TPU v7x, 32 devices: a whole 2x2x4 slice. The times are simulated.
32 devices in a mesh: groups: 2 (over y), dp: 4 (over z), tensor: 4 (over x, core).
Axes of the slice: x: 2, y: 2, z: 4, core: 2. Of those that a mesh axis runs over, the one named last changes fastest.
Arguments:
- acts: bfloat16 [2048, 8192], P(('groups', 'dp'), 'tensor'), parts along dimension 0, may hold values from -6 to 6
- output_gradient: bfloat16 [2048, 4096], P(('groups', 'dp'), 'tensor'), parts along dimension 0, may hold values from -6 to 6
- frozen_weight: bfloat16 [8192, 4096], P('tensor', 'dp'), may hold values from -0.09375 to 0.09375
- adapter_down_weights: bfloat16 [64, 16, 8192], P('dp', None, 'tensor'), may hold values from -0.25 to 0.25
- adapter_up_weights: bfloat16 [64, 16, 4096], P('dp', None, 'tensor'), may hold values from -0.09375 to 0.09375
- block_adapter_index: int32 [16], P('groups'), parts along dimension 0, may hold values from 0 to 63, as said below
- adapter_slot_index: int32 [64], replicated, may hold values from 0 to 63, each once
Outputs:
- in_grad: bfloat16 [2048, 8192], P(('groups', 'dp'), 'tensor'), parts along dimension 0
- owned_down: float32 [128, 16, 8192], P(('groups', 'dp'), None, 'tensor'), parts along dimension 0
- owned_up: float32 [128, 16, 4096], P(('groups', 'dp'), None, 'tensor'), parts along dimension 0
There are 2 independent parts, one for each index of `groups`. A program takes and returns all parts, laid end to end along the dimension named above; an argument that names none is the same for every part. Nothing has to cross between parts.
Inputs may be any that keep to these rules, and one draw needn't show every extreme that they name: `block_adapter_index`: never falls from one block to the next; blocks of one adapter stand together. `adapter_slot_index`: each slot is named once.
All inputs are finite; a program needn't handle non-finite values.
Results may differ from a plain program's by a relative error of at most 0.005.
Values may be sent and summed in bfloat16 or wider, within the bound.
A program may use at most 128 MiB of HBM per device.

v0:
```python
import jax
import jax.numpy as jnp
from jax import lax
from jax.sharding import PartitionSpec as P

BLOCK_TOKENS = 128


ADAPTER_SCALE = 2.0


def per_device(
    acts,
    output_gradient,
    frozen_weight,
    adapter_down_weights,
    adapter_up_weights,
    block_adapter_index,
    adapter_slot_index,
):
    tok_rows, in_cols = acts.shape
    out_cols = output_gradient.shape[1]
    blocks_dev = tok_rows // BLOCK_TOKENS
    own_index = lax.axis_index("dp")
    per_holder_sums = adapter_down_weights.shape[0]
    my_blocks = lax.dynamic_slice_in_dim(block_adapter_index, own_index * blocks_dev, blocks_dev)
    all_down, all_up = (
        lax.all_gather(adapter_down_weights, "dp", axis=0, tiled=True),
        lax.all_gather(adapter_up_weights, "dp", axis=0, tiled=True),
    )
    my_slots = adapter_slot_index[my_blocks]
    selected_down = all_down[my_slots]
    up_sel = all_up[my_slots]
    active_block_rows = acts.reshape(blocks_dev, BLOCK_TOKENS, in_cols)
    grad_blocks = output_gradient.reshape(blocks_dev, BLOCK_TOKENS, out_cols)
    down_portion = jnp.einsum(
        "ctx,cyx->cty", active_block_rows, selected_down, preferred_element_type=jnp.float32
    )
    up_part = jnp.einsum("bko,bro->bkr", grad_blocks, up_sel, preferred_element_type=jnp.float32)
    reduced_rank_output, back_rank = lax.psum((down_portion, up_part), "tensor")
    lowrank_b = reduced_rank_output.astype(jnp.bfloat16)
    backward_block = back_rank.astype(jnp.bfloat16)
    widened_gradient = ADAPTER_SCALE * jnp.einsum(
        "aex,axq->aeq", backward_block, selected_down, preferred_element_type=jnp.float32
    )
    widened_gradient = widened_gradient.reshape(tok_rows, in_cols)
    full_grad = lax.all_gather(output_gradient, "tensor", axis=1, tiled=True)
    in_grad = (
        widened_gradient
        + lax.dot_general(
            full_grad,
            lax.all_gather(frozen_weight, "dp", axis=1, tiled=True),
            (((1,), (1,)), ((), ())),
            preferred_element_type=jnp.float32,
        )
    ).astype(jnp.bfloat16)
    factor_matrix = ADAPTER_SCALE / BLOCK_TOKENS
    grad_down = (
        factor_matrix
        * jnp.einsum(
            "aqw,aqg->awg", backward_block, active_block_rows, preferred_element_type=jnp.float32
        )
    ).astype(jnp.bfloat16)
    grad_up = (
        factor_matrix
        * jnp.einsum("bkr,bko->bro", lowrank_b, grad_blocks, preferred_element_type=jnp.float32)
    ).astype(jnp.bfloat16)
    slot_range = jnp.arange(per_holder_sums, dtype=jnp.int32)
    base_slot = own_index * per_holder_sums
    piece_down = lax.all_gather(grad_down, "dp", axis=0, tiled=True)
    piece_up = lax.all_gather(grad_up, "dp", axis=0, tiled=True)
    slot_local = adapter_slot_index[block_adapter_index] - base_slot
    chooser = (slot_local[:, None] == slot_range[None, :]).astype(jnp.bfloat16)
    new_down = jnp.einsum("ns,nrd->srd", chooser, piece_down, preferred_element_type=jnp.float32)
    new_up = jnp.einsum("ns,nro->sro", chooser, piece_up, preferred_element_type=jnp.float32)
    return (in_grad, new_down, new_up)


def solution(mesh):
    return jax.shard_map(
        per_device,
        mesh=mesh,
        in_specs=(
            P(("groups", "dp"), "tensor"),
            P(("groups", "dp"), "tensor"),
            P("tensor", "dp"),
            P("dp", None, "tensor"),
            P("dp", None, "tensor"),
            P("groups"),
            P(),
        ),
        out_specs=(
            P(("groups", "dp"), "tensor"),
            P(("groups", "dp"), None, "tensor"),
            P(("groups", "dp"), None, "tensor"),
        ),
        check_vma=False,
    )
```

profile of v0, /device:TPU:3, one launch (start us, length us, event | category | flops | bytes accessed | tf_op | source)
XLA Modules:
  0.0 469.5 jit_solution(5545638649981728839)
XLA Ops:
  7.2 0.7 all-gather.5.cloned.1.call-update
  8.0 0.7 all-gather.7.cloned.1.call-update
  8.7 0.7 all-gather.9.cloned.1.call-update
  9.5 0.5 all-gather.11.cloned.1.call-update
  10.1 0.6 gather_fusion
  10.8 0.6 gather_fusion.3
  11.5 45.3 %all-gather.5.cloned.1.call-done = bf16[64,16,1024]{2,1,0:T(8,128)(2,1)} async-done(((bf16[16,16,1024]{2,1,0:T(8,128)(2,1)}), bf16[64,16,1024]{2,1,0:T(8,128)(2,1)}) %all-gather.5.cloned.1.call-update) | async-done | bytes 2097168 | tf_op jit(solution)/shard_map/all_gather | solution.py:29
  56.8 2.1 gather_fusion.1
  58.9 0.2 convolution_bitcast_fusion.1
  59.2 78.7 %all-gather.7.cloned.1.call-done = bf16[64,16,2048]{2,1,0:T(8,128)(2,1)} async-done(((bf16[16,16,2048]{2,1,0:T(8,128)(2,1)}), bf16[64,16,2048]{2,1,0:T(8,128)(2,1)}) %all-gather.7.cloned.1.call-update) | async-done | bytes 4194320 | tf_op jit(solution)/shard_map/all_gather | solution.py:28
  137.9 2.7 gather_fusion.2
  140.6 0.4 convolution_bitcast_fusion
  141.0 11.1 %all-reduce = (bf16[2,128,16]{1,2,0:T(8,128)(2,1)S(1)}, bf16[2,128,16]{1,2,0:T(8,128)(2,1)S(1)}) all-reduce(f32[2,128,16]{1,2,0:T(8,128)S(1)} %convolution_bitcast_fusion.1, f32[2,128,16]{1,2,0:T(8,128)S(1)} %convolution_bitcast_fusion), channel_id=1, replica_groups=mesh['groups'=2,'dp'=4,'tensor'=4] {'tensor'}, use_global_device_ids=true, to_apply=%region_0.0 | all-reduce | flops 8192 | bytes 49152 | tf_op jit(solution)/shard_map/psum | solution.py:40
  152.1 0.3 fusion.1
  152.3 12.1 %all_gather.22 = bf16[8,16,2048]{2,1,0:T(8,128)(2,1)S(1)} all-gather(bf16[2,16,2048]{2,1,0:T(8,128)(2,1)S(1)} %fusion.1), channel_id=1, replica_groups=mesh['groups'=2,'dp'=4,'tensor'=4] {'dp'}, dimensions={0}, use_global_device_ids=true | all-gather | bytes 655360 | tf_op jit(solution)/shard_map/all_gather | solution.py:70
  164.5 0.6 fusion.3
  165.0 2.5 copy.16
  167.6 0.2 fusion.2
  167.8 11.6 %all_gather.23 = bf16[8,16,1024]{2,1,0:T(8,128)(2,1)S(1)} all-gather(bf16[2,16,1024]{2,1,0:T(8,128)(2,1)S(1)} %fusion.2), channel_id=1, replica_groups=mesh['groups'=2,'dp'=4,'tensor'=4] {'dp'}, dimensions={0}, use_global_device_ids=true | all-gather | bytes 327680 | tf_op jit(solution)/shard_map/all_gather | solution.py:71
  179.4 0.4 fusion.5
  179.8 1.6 copy.17
  181.4 0.5 convolution_multiply_fusion
  181.9 269.2 %all-gather.11.cloned.1.call-done = bf16[2048,4096]{1,0:T(8,128)(2,1)} async-done(((bf16[2048,1024]{1,0:T(8,128)(2,1)}), bf16[2048,4096]{1,0:T(8,128)(2,1)}) %all-gather.11.cloned.1.call-update) | async-done | bytes 16777232 | tf_op jit(solution)/shard_map/all_gather | solution.py:52
  451.1 11.9 %fusion = bf16[256,2048]{1,0:T(8,128)(2,1)} fusion(f32[256,2048]{1,0:T(8,128)S(1)} %bitcast.31, bf16[256,4096]{1,0:T(8,128)(2,1)} %all-gather.9.cloned.1.call-done, bf16[2048,4096]{1,0:T(8,128)(2,1)} %all-gather.11.cloned.1.call-done), kind=kOutput, calls=%fused_computation.6 | convolution fusion | flops 4296015872 | bytes 22020096 | tf_op jit(solution)/shard_map/dot_general | solution.py:50
  (20 shorter events, 0.3 us)
Async XLA Ops:
  7.2 133.5 %copy-start = (bf16[256,2048]{1,0:T(8,128)(2,1)S(1)}, bf16[256,2048]{1,0:T(8,128)(2,1)}, u32[]{:S(2)}) copy-start(bf16[256,2048]{1,0:T(8,128)(2,1)} %param.7) | copy-start | bytes 3145732
  7.2 49.6 %all-gather.5.cloned.1.call-start = ((), (), s32[]{:S(2)}) async-start(), calls=%async_computation | async-start | bytes 2621440 | tf_op jit(solution)/shard_map/all_gather | solution.py:29
  7.9 130.0 %all-gather.7.cloned.1.call-start = ((), (), s32[]{:S(2)}) async-start(), calls=%async_computation.1 | async-start | bytes 5242880 | tf_op jit(solution)/shard_map/all_gather | solution.py:28
  8.7 173.2 %all-gather.9.cloned.1.call-start = ((), (), s32[]{:S(2)}) async-start(), calls=%async_computation.2 | async-start | bytes 2621440 | tf_op jit(solution)/shard_map/all_gather | solution.py:47
  9.4 0.7 copy-start.3
  9.4 0.7 copy-start.1
  9.4 49.5 %copy-start.2 = (bf16[256,1024]{1,0:T(8,128)(2,1)S(1)}, bf16[256,1024]{1,0:T(8,128)(2,1)}, u32[]{:S(2)}) copy-start(bf16[256,1024]{1,0:T(8,128)(2,1)} %param.8) | copy-start | bytes 1572868
  9.4 441.7 %all-gather.11.cloned.1.call-start = ((), (), s32[]{:S(2)}) async-start(), calls=%async_computation.3 | async-start | bytes 20971520 | tf_op jit(solution)/shard_map/all_gather | solution.py:52
Sparse Core Ops, SparseCore 0:
  9.6 47.1 all-gather.4
  58.4 79.4 all-gather.6
  139.4 20.6 all-gather.8
  161.6 289.4 all-gather.10
where the time goes:
time: 471 us; the launch traced here: 470 us
  waiting for transfers between devices  396 us (84%)
  blocking collectives  34.8 us (7%)
  matrix products  14.4 us (3%)
  between operations  13.9 us (3%)
  local copies, waits for them, and re-layouts  10.3 us (2%)
    all_gather x1, waiting for transfers between devices, per_device(): lax.all_gather(frozen_weight, 'dp', axis=1, tiled=True)  269 us
    all_gather x1, waiting for transfers between devices, per_device(): lax.all_gather(adapter_down_weights, 'dp', axis=0, tiled=True)  78.7 us
    all_gather x1, waiting for transfers between devices, per_device(): lax.all_gather(adapter_up_weights, 'dp', axis=0, tiled=True)  45.3 us
    all_gather x1, blocking collectives, per_device(): piece_down = lax.all_gather(grad_down, 'dp', axis=0, tiled=True)  12.1 us
    dot_general x1, matrix products, per_device(): lax.dot_general(full_grad, lax.all_gather(frozen_weight, 'dp', axis=1, ti...  11.9 us
    all_gather x1, blocking collectives, per_device(): piece_up = lax.all_gather(grad_up, 'dp', axis=0, tiled=True)  11.6 us
    psum x1, blocking collectives, per_device(): reduced_rank_output, back_rank = lax.psum((down_portion, up_part), 'tensor')  11.1 us
  transfers between devices with their start and end apart: 4, of which 3 were waited for; matrix products, arithmetic and copies ran while one was open for 3% of the time, Pallas kernels for 0%

commit v1 on v0

--- a/solution.py
+++ b/solution.py
@@ -1,12 +1,274 @@
+import functools
+
 import jax
 import jax.numpy as jnp
 from jax import lax
+from jax.experimental import pallas as pl
+from jax.experimental.pallas import tpu as pltpu
 from jax.sharding import PartitionSpec as P
 
 BLOCK_TOKENS = 128
 
 
 ADAPTER_SCALE = 2.0
+
+
+MESH = pl.DeviceIdType.MESH
+NT = (((1,), (1,)), ((), ()))
+NN = (((1,), (0,)), ((), ()))
+RANK = 16
+
+
+def chain_order(dp):
+    table = []
+    for own in range(dp):
+        up, down = list(range(dp - 1, own, -1)), list(range(own))
+        first, second = (up, down) if len(up) >= len(down) else (down, up)
+        merged = []
+        while first or second:
+            if first:
+                merged.append(first.pop(0))
+            if second:
+                merged.append(second.pop(0))
+        table.append(merged)
+    return table
+
+
+def fused_kernel(
+    dp, tensor, chunks,
+    block_ref, slot_ref, acts_ref, og_ref, w_ref, down_ref, up_ref,
+    grad_ref, own_down_ref, own_up_ref,
+    og_all, partial, arrived, total, sel_send, sel_recv, rank_mine, rank_recv, pieces,
+    og_send, og_near, og_far, og_relay, og_recv,
+    sel_ssem, sel_rsem, rank_ssem, rank_rsem, piece_ssem, piece_rsem, part_ssem, part_rsem,
+):
+    d, t = lax.axis_index("dp"), lax.axis_index("tensor")
+    rows, in_cols = acts_ref.shape
+    out_cols = og_ref.shape[1]
+    nblk = rows // BLOCK_TOKENS
+    nslot = down_ref.shape[0]
+    quarter = rows // tensor
+    width = in_cols // chunks
+    sib, across = t + 1 - 2 * (t % 2), (t + 2) % tensor
+    across_sib = across + 1 - 2 * (across % 2)
+
+    table = chain_order(dp)
+    order = []
+    for k in range(dp - 1):
+        at = jnp.int32(table[0][k])
+        for i in range(1, dp):
+            at = jnp.where(d == i, table[i][k], at)
+        order.append(at)
+
+    def wait(ref, sem):
+        pltpu.make_async_copy(ref, ref, sem).wait()
+
+    def send(src, dst, ssem, rsem, to):
+        copy = pltpu.make_async_remote_copy(
+            src_ref=src, dst_ref=dst, send_sem=ssem, recv_sem=rsem, device_id=to, device_id_type=MESH
+        )
+        copy.start()
+        return copy
+
+    barrier = pltpu.get_barrier_semaphore()
+    for i in range(1, dp * tensor):
+        peer = (d * tensor + t + i) % (dp * tensor)
+        pl.semaphore_signal(
+            barrier, inc=1, device_id={"dp": peer // tensor, "tensor": peer % tensor}, device_id_type=MESH
+        )
+    pl.semaphore_wait(barrier, dp * tensor - 1)
+
+    def og_rows(q):
+        return pl.ds(pl.multiple_of(q * quarter, quarter), quarter)
+
+    stays = [jnp.logical_and(t == d, t == q) for q in range(tensor)]
+    for q in range(tensor):
+        src, dst = og_ref.at[og_rows(q)], og_all.at[d, og_rows(q)]
+
+        @pl.when(stays[q])
+        def _():
+            pltpu.make_async_copy(src, dst, og_recv.at[d, q]).start()
+
+        @pl.when(jnp.logical_not(stays[q]))
+        def _():
+            send(src, dst, og_send.at[q], og_recv.at[d, q], {"dp": t, "tensor": q})
+
+    slots = [slot_ref[block_ref[b]] for b in range(dp * nblk)]
+    for b in range(dp * nblk):
+        here = slots[b] - d * nslot
+        own = jnp.logical_and(here >= 0, here < nslot)
+        at = jnp.clip(here, 0, nslot - 1)
+        dn, up = down_ref[at], up_ref[at]
+        r = pl.ds((b % nblk) * RANK, RANK)
+        sel_send[b // nblk, r, :in_cols] = jnp.where(own, dn, jnp.zeros_like(dn))
+        sel_send[b // nblk, r, in_cols:] = jnp.where(own, up, jnp.zeros_like(up))
+    waits = []
+    for j in range(1, dp):
+        peer = (d + j) % dp
+        waits.append(send(sel_send.at[peer], sel_recv.at[d], sel_ssem.at[j - 1], sel_rsem.at[d], {"dp": peer}))
+
+    fetch_order = order + [d]
+    for k, row in enumerate(fetch_order):
+        piece = og_all.at[row, og_rows(t)]
+        wait(piece, og_recv.at[row, t])
+        waits.append(send(piece, piece, og_far.at[k], og_recv.at[row, t], {"tensor": across}))
+        waits.append(send(piece, piece, og_near.at[k], og_recv.at[row, t], {"tensor": sib}))
+
+    sel = sel_send[d]
+    for j in range(1, dp):
+        peer = (d + j) % dp
+        wait(sel_recv.at[peer], sel_rsem.at[peer])
+        sel = sel + sel_recv[peer]
+    sel_recv[d] = sel
+    for c in range(nblk):
+        r, tok = pl.ds(c * RANK, RANK), pl.ds(c * BLOCK_TOKENS, BLOCK_TOKENS)
+        low = lax.dot_general(sel_recv[d, r, :in_cols], acts_ref[tok, :], NT, preferred_element_type=jnp.float32)
+        back = lax.dot_general(sel_recv[d, r, in_cols:], og_ref[tok, :], NT, preferred_element_type=jnp.float32)
+        rank_mine[pl.ds(c * RANK, RANK), :] = low
+        rank_mine[pl.ds((nblk + c) * RANK, RANK), :] = back
+    for j in range(1, tensor):
+        peer = (t + j) % tensor
+        waits.append(send(rank_mine, rank_recv.at[t], rank_ssem.at[j - 1], rank_rsem.at[t], {"tensor": peer}))
+
+    for k, row in enumerate(fetch_order):
+        piece = og_all.at[row, og_rows(across)]
+        wait(piece, og_recv.at[row, across])
+        waits.append(send(piece, piece, og_relay.at[k], og_recv.at[row, across], {"tensor": sib}))
+
+    rank = rank_mine[...]
+    for j in range(1, tensor):
+        peer = (t + j) % tensor
+        wait(rank_recv.at[peer], rank_rsem.at[peer])
+        rank = rank + rank_recv[peer]
+    rank_b = rank.astype(jnp.bfloat16)
+    factor = ADAPTER_SCALE / BLOCK_TOKENS
+    back_t = []
+    for c in range(nblk):
+        tok = pl.ds(c * BLOCK_TOKENS, BLOCK_TOKENS)
+        low_b = rank_b[c * RANK:(c + 1) * RANK, :]
+        back_b = rank_b[(nblk + c) * RANK:(nblk + c + 1) * RANK, :]
+        at = pl.ds(pl.multiple_of((d * nblk + c) * RANK, RANK), RANK)
+        pieces[at, :in_cols] = (
+            factor * lax.dot_general(back_b, acts_ref[tok, :], NN, preferred_element_type=jnp.float32)
+        ).astype(jnp.bfloat16)
+        pieces[at, in_cols:] = (
+            factor * lax.dot_general(low_b, og_ref[tok, :], NN, preferred_element_type=jnp.float32)
+        ).astype(jnp.bfloat16)
+        back_t.append(rank[(nblk + c) * RANK:(nblk + c + 1) * RANK, :].T.astype(jnp.bfloat16))
+    mine = pl.ds(pl.multiple_of(d * nblk * RANK, nblk * RANK), nblk * RANK)
+    for j in range(1, dp):
+        peer = (d + j) % dp
+        waits.append(send(pieces.at[mine], pieces.at[mine], piece_ssem.at[j - 1], piece_rsem.at[d], {"dp": peer}))
+
+    def product(row, c):
+        tile = w_ref[pl.ds(pl.multiple_of(c * width, width), width), :]
+        return lax.dot_general(og_all[row], tile, NT, preferred_element_type=jnp.float32)
+
+    for k, row in enumerate(order):
+        for q in (sib, across_sib):
+            wait(og_all.at[row, og_rows(q)], og_recv.at[row, q])
+        upward = row > d
+        fed = jnp.logical_or(jnp.logical_and(upward, d > 0), jnp.logical_and(row < d, d < dp - 1))
+        to = jnp.where(upward, d + 1, d - 1)
+        lands = jnp.where(row == d - 1, dp, row)
+
+        @pl.loop(0, chunks)
+        def _(c):
+            total[...] = product(row, c)
+
+            @pl.when(fed)
+            def _():
+                wait(arrived.at[row, c], part_rsem.at[row, c])
+                total[...] += arrived[row, c].astype(jnp.float32)
+
+            partial[k, c] = total[...].astype(jnp.bfloat16)
+            send(partial.at[k, c], arrived.at[lands, c], part_ssem.at[k, c], part_rsem.at[lands, c], {"dp": to})
+
+    for j in range(1, dp):
+        peer = (d + j) % dp
+        theirs = pl.ds(pl.multiple_of(peer * nblk * RANK, nblk * RANK), nblk * RANK)
+        wait(pieces.at[theirs], piece_rsem.at[peer])
+    shape = (nslot * RANK, dp * nblk * RANK)
+    line, column = lax.broadcasted_iota(jnp.int32, shape, 0), lax.broadcasted_iota(jnp.int32, shape, 1)
+    goal = jnp.full(shape, -1, jnp.int32)
+    for b in range(dp * nblk):
+        goal = jnp.where(column // RANK == b, (slots[b] - d * nslot) * RANK + column % RANK, goal)
+    chooser = jnp.where(goal == line, 1.0, 0.0).astype(jnp.bfloat16)
+    own_down_ref[...] = lax.dot_general(chooser, pieces[:, :in_cols], NN, preferred_element_type=jnp.float32)
+    own_up_ref[...] = lax.dot_general(chooser, pieces[:, in_cols:], NN, preferred_element_type=jnp.float32)
+
+    for q in (sib, across_sib):
+        wait(og_all.at[d, og_rows(q)], og_recv.at[d, q])
+    for c in range(chunks):
+        cols = pl.ds(c * width, width)
+        total[...] = product(d, c)
+        for i in range(nblk):
+            tok = pl.ds(i * BLOCK_TOKENS, BLOCK_TOKENS)
+            total[tok, :] += ADAPTER_SCALE * lax.dot_general(
+                back_t[i], sel_recv[d, pl.ds(i * RANK, RANK), cols], NN, preferred_element_type=jnp.float32
+            )
+
+        @pl.when(d > 0)
+        def _():
+            wait(arrived.at[d, c], part_rsem.at[d, c])
+            total[...] += arrived[d, c].astype(jnp.float32)
+
+        @pl.when(d < dp - 1)
+        def _():
+            wait(arrived.at[dp, c], part_rsem.at[dp, c])
+            total[...] += arrived[dp, c].astype(jnp.float32)
+
+        grad_ref[:, cols] = total[...].astype(jnp.bfloat16)
+
+    for copy in waits:
+        copy.wait_send()
+    for q in range(tensor):
+        @pl.when(jnp.logical_not(stays[q]))
+        def _():
+            wait(og_ref.at[og_rows(q)], og_send.at[q])
+    for k in range(dp - 1):
+        for c in range(chunks):
+            wait(partial.at[k, c], part_ssem.at[k, c])
+
+
+def fused(dp, tensor, acts, og, w, down, up, blocks, slots):
+    rows, in_cols = acts.shape
+    out_cols = og.shape[1]
+    nslot, nblk, chunks = down.shape[0], rows // BLOCK_TOKENS, 4
+    width = in_cols // chunks
+    vmem, smem = pl.BlockSpec(memory_space=pltpu.VMEM), pl.BlockSpec(memory_space=pltpu.SMEM)
+    dma = pltpu.SemaphoreType.DMA
+    grad, own_down, own_up = pl.pallas_call(
+        functools.partial(fused_kernel, dp, tensor, chunks),
+        out_shape=(
+            jax.ShapeDtypeStruct((rows, in_cols), jnp.bfloat16),
+            jax.ShapeDtypeStruct((nslot * RANK, in_cols), jnp.float32),
+            jax.ShapeDtypeStruct((nslot * RANK, out_cols), jnp.float32),
+        ),
+        in_specs=[smem, smem] + [vmem] * 5,
+        out_specs=(vmem, vmem, vmem),
+        scratch_shapes=[
+            pltpu.VMEM((dp, rows, w.shape[1]), jnp.bfloat16),
+            pltpu.VMEM((dp - 1, chunks, rows, width), jnp.bfloat16),
+            pltpu.VMEM((dp + 1, chunks, rows, width), jnp.bfloat16),
+            pltpu.VMEM((rows, width), jnp.float32),
+            pltpu.VMEM((dp, nblk * RANK, in_cols + out_cols), jnp.bfloat16),
+            pltpu.VMEM((dp, nblk * RANK, in_cols + out_cols), jnp.bfloat16),
+            pltpu.VMEM((2 * nblk * RANK, BLOCK_TOKENS), jnp.float32),
+            pltpu.VMEM((tensor, 2 * nblk * RANK, BLOCK_TOKENS), jnp.float32),
+            pltpu.VMEM((dp * nblk * RANK, in_cols + out_cols), jnp.bfloat16),
+            dma((tensor,)), dma((dp,)), dma((dp,)), dma((dp,)), dma((dp, tensor)),
+            dma((dp - 1,)), dma((dp,)), dma((tensor - 1,)), dma((tensor,)),
+            dma((dp - 1,)), dma((dp,)), dma((dp - 1, chunks)), dma((dp + 1, chunks)),
+        ],
+        compiler_params=pltpu.CompilerParams(
+            collective_id=0, has_side_effects=True, vmem_limit_bytes=48 * 1024 * 1024
+        ),
+        cost_estimate=pl.CostEstimate(
+            flops=2 * dp * rows * in_cols * w.shape[1], bytes_accessed=12 * 1024 * 1024, transcendentals=0
+        ),
+    )(blocks, slots, acts, og, w, down, up)
+    return grad, own_down.reshape(nslot, RANK, in_cols), own_up.reshape(nslot, RANK, out_cols)
 
 
 def per_device(
@@ -77,8 +339,15 @@
 
 
 def solution(mesh):
+    dp, tensor = mesh.shape["dp"], mesh.shape["tensor"]
+
+    def step(acts, og, w, down, up, blocks, slots):
+        if dp == tensor == 4:
+            return fused(dp, tensor, acts, og, w, down, up, blocks, slots)
+        return per_device(acts, og, w, down, up, blocks, slots)
+
     return jax.shard_map(
-        per_device,
+        step,
         mesh=mesh,
         in_specs=(
             P(("groups", "dp"), "tensor"),

time: 471 us -> 146 us (0.31)
  the two profiles are of different devices: /device:TPU:3 before, /device:TPU:17 now
where the time goes in v1:
time: 146 us
  Pallas kernels  135 us (92%)
  local copies, waits for them, and re-layouts  10.1 us (7%)
    pallas_call x1, Pallas kernels, fused(): pl.pallas_call(functools.partial(fused_kernel, dp, tensor, chunks), out_s...  135 us
    unnamed x17, local copies, waits for them, and re-layouts  10.1 us

profile of v1, /device:TPU:17, one launch (start us, length us, event | category | flops | bytes accessed | tf_op | source)
XLA Modules:
  0.0 146.0 jit_solution(11644814613710104963)
XLA Ops:
  0.6 0.0 copy-start
  0.6 1.2 copy-done
  1.9 0.0 copy-start.1
  1.9 1.2 copy-done.1
  3.1 0.0 copy-start.2
  3.1 1.0 copy-done.2
  4.1 0.0 copy-start.3
  4.1 1.0 copy-done.3
  5.2 0.0 copy-start.4
  5.2 0.7 copy-done.4
  5.8 0.0 copy-start.5
  5.8 0.7 copy-done.5
  6.5 135.2 %shard_map.94 = (bf16[256,2048]{1,0:T(8,128)(2,1)S(1)}, f32[256,2048]{1,0:T(8,128)}, f32[256,1024]{1,0:T(8,128)S(1)}) custom-call(s32[8]{0:T(128)S(1)} %copy-done.4, s32[64]{0:T(128)S(1)} %copy-done.5, bf16[256,2048]{1,0:T(8,128)(2,1)S(1)} %copy-done, bf16[256,1024]{1,0:T(8,128)(2,1)S(1)} %copy-done.2, bf16[2048,1024]{1,0:T(8,128)(2,1)} %w_ref.1, ...), custom_call_target="tpu_custom_call" | custom-call | flops 4294967296 | bytes 12582912 | tf_op jit(solution)/shard_map/pallas_call | solution.py:241
  141.7 0.0 copy-start.6
  141.7 1.0 copy.13
  142.7 1.0 copy-done.6
  143.7 1.3 copy.14
  145.0 1.0 copy.15
Async XLA Ops:
  0.6 1.2 copy-start
  1.9 1.2 copy-start.1
  3.1 1.0 copy-start.2
  4.1 1.0 copy-start.3
  5.2 0.7 copy-start.4
  5.8 0.7 copy-start.5
  141.7 2.0 %copy-start.6 = (f32[256,2048]{1,0:T(8,128)S(1)}, f32[256,2048]{1,0:T(8,128)}, u32[]{:S(2)}) copy-start(f32[256,2048]{1,0:T(8,128)} %get-tuple-element.7) | copy-start | bytes 6291460

commit v2 on v1

--- a/solution.py
+++ b/solution.py
@@ -36,21 +36,22 @@
 
 def fused_kernel(
     dp, tensor, chunks,
-    block_ref, slot_ref, acts_ref, og_ref, w_ref, down_ref, up_ref,
+    block_ref, slot_ref, acts_hbm, og_hbm, w_hbm, down_hbm, up_hbm,
     grad_ref, own_down_ref, own_up_ref,
-    og_all, partial, arrived, total, sel_send, sel_recv, rank_mine, rank_recv, pieces,
-    og_send, og_near, og_far, og_relay, og_recv,
+    acts_ref, og_ref, w_ref, down_ref, up_ref,
+    og_all, partial, arrived, total, own_total, sel_send, sel_recv, rank_mine, rank_recv, pieces,
+    load_sem, og_send, og_near, og_far, og_relay, og_recv,
     sel_ssem, sel_rsem, rank_ssem, rank_rsem, piece_ssem, piece_rsem, part_ssem, part_rsem,
 ):
     d, t = lax.axis_index("dp"), lax.axis_index("tensor")
     rows, in_cols = acts_ref.shape
-    out_cols = og_ref.shape[1]
     nblk = rows // BLOCK_TOKENS
     nslot = down_ref.shape[0]
-    quarter = rows // tensor
+    quarter, half = rows // tensor, rows // 2
     width = in_cols // chunks
     sib, across = t + 1 - 2 * (t % 2), (t + 2) % tensor
     across_sib = across + 1 - 2 * (across % 2)
+    x = t // 2
 
     table = chain_order(dp)
     order = []
@@ -70,6 +71,15 @@
         copy.start()
         return copy
 
+    loads = [
+        pltpu.make_async_copy(src, dst, load_sem.at[i])
+        for i, (src, dst) in enumerate(
+            ((down_hbm, down_ref), (up_hbm, up_ref), (w_hbm, w_ref), (acts_hbm, acts_ref), (og_hbm, og_ref))
+        )
+    ]
+    for load in loads:
+        load.start()
+
     barrier = pltpu.get_barrier_semaphore()
     for i in range(1, dp * tensor):
         peer = (d * tensor + t + i) % (dp * tensor)
@@ -83,7 +93,7 @@
 
     stays = [jnp.logical_and(t == d, t == q) for q in range(tensor)]
     for q in range(tensor):
-        src, dst = og_ref.at[og_rows(q)], og_all.at[d, og_rows(q)]
+        src, dst = og_hbm.at[og_rows(q)], og_all.at[d, og_rows(q)]
 
         @pl.when(stays[q])
         def _():
@@ -94,6 +104,8 @@
             send(src, dst, og_send.at[q], og_recv.at[d, q], {"dp": t, "tensor": q})
 
     slots = [slot_ref[block_ref[b]] for b in range(dp * nblk)]
+    loads[0].wait()
+    loads[1].wait()
     for b in range(dp * nblk):
         here = slots[b] - d * nslot
         own = jnp.logical_and(here >= 0, here < nslot)
@@ -103,17 +115,58 @@
         sel_send[b // nblk, r, :in_cols] = jnp.where(own, dn, jnp.zeros_like(dn))
         sel_send[b // nblk, r, in_cols:] = jnp.where(own, up, jnp.zeros_like(up))
     waits = []
-    for j in range(1, dp):
-        peer = (d + j) % dp
-        waits.append(send(sel_send.at[peer], sel_recv.at[d], sel_ssem.at[j - 1], sel_rsem.at[d], {"dp": peer}))
 
     fetch_order = order + [d]
     for k, row in enumerate(fetch_order):
         piece = og_all.at[row, og_rows(t)]
         wait(piece, og_recv.at[row, t])
+        waits.append(send(piece, piece, og_near.at[k], og_recv.at[row, t], {"tensor": sib}))
         waits.append(send(piece, piece, og_far.at[k], og_recv.at[row, t], {"tensor": across}))
-        waits.append(send(piece, piece, og_near.at[k], og_recv.at[row, t], {"tensor": sib}))
-
+
+    for j in range(1, dp):
+        peer = (d + j) % dp
+        waits.append(send(sel_send.at[peer], sel_recv.at[d], sel_ssem.at[j - 1], sel_rsem.at[d], {"dp": peer}))
+
+    def half_rows(h):
+        place = x if h == 0 else 1 - x
+        return pl.ds(pl.multiple_of(place * half, half), half)
+
+    def relay_sums(k, h):
+        row = order[k]
+        wait(og_all.at[row, og_rows(sib if h == 0 else across_sib)], og_recv.at[row, sib if h == 0 else across_sib])
+        upward = row > d
+        fed = jnp.logical_or(jnp.logical_and(upward, d > 0), jnp.logical_and(row < d, d < dp - 1))
+        to = jnp.where(upward, d + 1, d - 1)
+        lands = jnp.where(row == d - 1, dp, row)
+
+        @pl.loop(0, chunks)
+        def _(c):
+            i = h * chunks + c
+            tile = w_ref[pl.ds(pl.multiple_of(c * width, width), width), :]
+            total[...] = lax.dot_general(
+                og_all[row, half_rows(h), :], tile, NT, preferred_element_type=jnp.float32
+            )
+
+            @pl.when(fed)
+            def _():
+                wait(arrived.at[row, i], part_rsem.at[row, i])
+                total[...] += arrived[row, i].astype(jnp.float32)
+
+            partial[k, i] = total[...].astype(jnp.bfloat16)
+            send(partial.at[k, i], arrived.at[lands, i], part_ssem.at[k, i], part_rsem.at[lands, i], {"dp": to})
+
+    loads[2].wait()
+    relay_sums(0, 0)
+
+    for k, row in enumerate(fetch_order):
+        piece = og_all.at[row, og_rows(across)]
+        wait(piece, og_recv.at[row, across])
+        waits.append(send(piece, piece, og_relay.at[k], og_recv.at[row, across], {"tensor": sib}))
+
+    relay_sums(1, 0)
+
+    loads[3].wait()
+    loads[4].wait()
     sel = sel_send[d]
     for j in range(1, dp):
         peer = (d + j) % dp
@@ -130,10 +183,7 @@
         peer = (t + j) % tensor
         waits.append(send(rank_mine, rank_recv.at[t], rank_ssem.at[j - 1], rank_rsem.at[t], {"tensor": peer}))
 
-    for k, row in enumerate(fetch_order):
-        piece = og_all.at[row, og_rows(across)]
-        wait(piece, og_recv.at[row, across])
-        waits.append(send(piece, piece, og_relay.at[k], og_recv.at[row, across], {"tensor": sib}))
+    relay_sums(2, 0)
 
     rank = rank_mine[...]
     for j in range(1, tensor):
@@ -147,87 +197,94 @@
         tok = pl.ds(c * BLOCK_TOKENS, BLOCK_TOKENS)
         low_b = rank_b[c * RANK:(c + 1) * RANK, :]
         back_b = rank_b[(nblk + c) * RANK:(nblk + c + 1) * RANK, :]
-        at = pl.ds(pl.multiple_of((d * nblk + c) * RANK, RANK), RANK)
-        pieces[at, :in_cols] = (
+        pieces[d, pl.ds(c * RANK, RANK), :in_cols] = (
             factor * lax.dot_general(back_b, acts_ref[tok, :], NN, preferred_element_type=jnp.float32)
         ).astype(jnp.bfloat16)
-        pieces[at, in_cols:] = (
+        pieces[d, pl.ds(c * RANK, RANK), in_cols:] = (
             factor * lax.dot_general(low_b, og_ref[tok, :], NN, preferred_element_type=jnp.float32)
         ).astype(jnp.bfloat16)
         back_t.append(rank[(nblk + c) * RANK:(nblk + c + 1) * RANK, :].T.astype(jnp.bfloat16))
-    mine = pl.ds(pl.multiple_of(d * nblk * RANK, nblk * RANK), nblk * RANK)
-    for j in range(1, dp):
-        peer = (d + j) % dp
-        waits.append(send(pieces.at[mine], pieces.at[mine], piece_ssem.at[j - 1], piece_rsem.at[d], {"dp": peer}))
-
-    def product(row, c):
-        tile = w_ref[pl.ds(pl.multiple_of(c * width, width), width), :]
-        return lax.dot_general(og_all[row], tile, NT, preferred_element_type=jnp.float32)
-
-    for k, row in enumerate(order):
-        for q in (sib, across_sib):
-            wait(og_all.at[row, og_rows(q)], og_recv.at[row, q])
-        upward = row > d
-        fed = jnp.logical_or(jnp.logical_and(upward, d > 0), jnp.logical_and(row < d, d < dp - 1))
-        to = jnp.where(upward, d + 1, d - 1)
-        lands = jnp.where(row == d - 1, dp, row)
-
-        @pl.loop(0, chunks)
-        def _(c):
-            total[...] = product(row, c)
-
-            @pl.when(fed)
-            def _():
-                wait(arrived.at[row, c], part_rsem.at[row, c])
-                total[...] += arrived[row, c].astype(jnp.float32)
-
-            partial[k, c] = total[...].astype(jnp.bfloat16)
-            send(partial.at[k, c], arrived.at[lands, c], part_ssem.at[k, c], part_rsem.at[lands, c], {"dp": to})
-
-    for j in range(1, dp):
-        peer = (d + j) % dp
-        theirs = pl.ds(pl.multiple_of(peer * nblk * RANK, nblk * RANK), nblk * RANK)
-        wait(pieces.at[theirs], piece_rsem.at[peer])
-    shape = (nslot * RANK, dp * nblk * RANK)
-    line, column = lax.broadcasted_iota(jnp.int32, shape, 0), lax.broadcasted_iota(jnp.int32, shape, 1)
-    goal = jnp.full(shape, -1, jnp.int32)
-    for b in range(dp * nblk):
-        goal = jnp.where(column // RANK == b, (slots[b] - d * nslot) * RANK + column % RANK, goal)
-    chooser = jnp.where(goal == line, 1.0, 0.0).astype(jnp.bfloat16)
-    own_down_ref[...] = lax.dot_general(chooser, pieces[:, :in_cols], NN, preferred_element_type=jnp.float32)
-    own_up_ref[...] = lax.dot_general(chooser, pieces[:, in_cols:], NN, preferred_element_type=jnp.float32)
+
+    def pass_on(j, take, give):
+        for way, (has, more, step) in enumerate(((d >= j, d < dp - 1, 1), (d + j < dp, d > 0, -1))):
+            at = jnp.clip(d - step * j, 0, dp - 1)
+
+            if take:
+                @pl.when(has)
+                def _():
+                    wait(pieces.at[at], piece_rsem.at[at])
+
+            if give is not None:
+                @pl.when(jnp.logical_and(has, more))
+                def _():
+                    if give:
+                        send(
+                            pieces.at[at], pieces.at[at], piece_ssem.at[way, j], piece_rsem.at[at],
+                            {"dp": jnp.clip(d + step, 0, dp - 1)},
+                        )
+                    else:
+                        wait(pieces.at[at], piece_ssem.at[way, j])
+
+    pass_on(0, False, True)
+    for k in range(dp - 1):
+        relay_sums(k, 1)
+        pass_on(k + 1, True, True if k + 1 < dp - 1 else None)
 
     for q in (sib, across_sib):
         wait(og_all.at[d, og_rows(q)], og_recv.at[d, q])
     for c in range(chunks):
         cols = pl.ds(c * width, width)
-        total[...] = product(d, c)
+        own_total[:, cols] = lax.dot_general(
+            og_all[d], w_ref[cols, :], NT, preferred_element_type=jnp.float32
+        )
         for i in range(nblk):
             tok = pl.ds(i * BLOCK_TOKENS, BLOCK_TOKENS)
-            total[tok, :] += ADAPTER_SCALE * lax.dot_general(
+            own_total[tok, cols] += ADAPTER_SCALE * lax.dot_general(
                 back_t[i], sel_recv[d, pl.ds(i * RANK, RANK), cols], NN, preferred_element_type=jnp.float32
             )
 
-        @pl.when(d > 0)
-        def _():
-            wait(arrived.at[d, c], part_rsem.at[d, c])
-            total[...] += arrived[d, c].astype(jnp.float32)
-
-        @pl.when(d < dp - 1)
-        def _():
-            wait(arrived.at[dp, c], part_rsem.at[dp, c])
-            total[...] += arrived[dp, c].astype(jnp.float32)
-
-        grad_ref[:, cols] = total[...].astype(jnp.bfloat16)
+    shape = (nslot * RANK, nblk * RANK)
+    line, column = lax.broadcasted_iota(jnp.int32, shape, 0), lax.broadcasted_iota(jnp.int32, shape, 1)
+    choosers = []
+    for r in range(dp):
+        goal = jnp.full(shape, -1, jnp.int32)
+        for b in range(nblk):
+            goal = jnp.where(
+                column // RANK == b, (slots[r * nblk + b] - d * nslot) * RANK + column % RANK, goal
+            )
+        choosers.append(jnp.where(goal == line, 1.0, 0.0).astype(jnp.bfloat16))
+    chooser = jnp.concatenate(choosers, axis=1)
+    all_pieces = pieces[...].reshape(dp * nblk * RANK, pieces.shape[2])
+    own_down_ref[...] = lax.dot_general(chooser, all_pieces[:, :in_cols], NN, preferred_element_type=jnp.float32)
+    own_up_ref[...] = lax.dot_general(chooser, all_pieces[:, in_cols:], NN, preferred_element_type=jnp.float32)
+
+    for h in range(2):
+        for c in range(chunks):
+            i, cols = h * chunks + c, pl.ds(c * width, width)
+            spot = half_rows(h)
+
+            @pl.when(d > 0)
+            def _():
+                wait(arrived.at[d, i], part_rsem.at[d, i])
+                own_total[spot, cols] += arrived[d, i].astype(jnp.float32)
+
+            @pl.when(d < dp - 1)
+            def _():
+                wait(arrived.at[dp, i], part_rsem.at[dp, i])
+                own_total[spot, cols] += arrived[dp, i].astype(jnp.float32)
+
+            grad_ref[spot, cols] = own_total[spot, cols].astype(jnp.bfloat16)
 
     for copy in waits:
         copy.wait_send()
+    for j in range(dp - 1):
+        pass_on(j, False, False)
     for q in range(tensor):
         @pl.when(jnp.logical_not(stays[q]))
         def _():
             wait(og_ref.at[og_rows(q)], og_send.at[q])
     for k in range(dp - 1):
-        for c in range(chunks):
+        for c in range(2 * chunks):
             wait(partial.at[k, c], part_ssem.at[k, c])
 
 
@@ -235,8 +292,9 @@
     rows, in_cols = acts.shape
     out_cols = og.shape[1]
     nslot, nblk, chunks = down.shape[0], rows // BLOCK_TOKENS, 4
-    width = in_cols // chunks
+    width, half = in_cols // chunks, rows // 2
     vmem, smem = pl.BlockSpec(memory_space=pltpu.VMEM), pl.BlockSpec(memory_space=pltpu.SMEM)
+    hbm = pl.BlockSpec(memory_space=pltpu.HBM)
     dma = pltpu.SemaphoreType.DMA
     grad, own_down, own_up = pl.pallas_call(
         functools.partial(fused_kernel, dp, tensor, chunks),
@@ -245,21 +303,27 @@
             jax.ShapeDtypeStruct((nslot * RANK, in_cols), jnp.float32),
             jax.ShapeDtypeStruct((nslot * RANK, out_cols), jnp.float32),
         ),
-        in_specs=[smem, smem] + [vmem] * 5,
+        in_specs=[smem, smem] + [hbm] * 5,
         out_specs=(vmem, vmem, vmem),
         scratch_shapes=[
+            pltpu.VMEM(acts.shape, jnp.bfloat16),
+            pltpu.VMEM(og.shape, jnp.bfloat16),
+            pltpu.VMEM(w.shape, jnp.bfloat16),
+            pltpu.VMEM(down.shape, jnp.bfloat16),
+            pltpu.VMEM(up.shape, jnp.bfloat16),
             pltpu.VMEM((dp, rows, w.shape[1]), jnp.bfloat16),
-            pltpu.VMEM((dp - 1, chunks, rows, width), jnp.bfloat16),
-            pltpu.VMEM((dp + 1, chunks, rows, width), jnp.bfloat16),
-            pltpu.VMEM((rows, width), jnp.float32),
+            pltpu.VMEM((dp - 1, 2 * chunks, half, width), jnp.bfloat16),
+            pltpu.VMEM((dp + 1, 2 * chunks, half, width), jnp.bfloat16),
+            pltpu.VMEM((half, width), jnp.float32),
+            pltpu.VMEM((rows, in_cols), jnp.float32),
             pltpu.VMEM((dp, nblk * RANK, in_cols + out_cols), jnp.bfloat16),
             pltpu.VMEM((dp, nblk * RANK, in_cols + out_cols), jnp.bfloat16),
             pltpu.VMEM((2 * nblk * RANK, BLOCK_TOKENS), jnp.float32),
             pltpu.VMEM((tensor, 2 * nblk * RANK, BLOCK_TOKENS), jnp.float32),
-            pltpu.VMEM((dp * nblk * RANK, in_cols + out_cols), jnp.bfloat16),
-            dma((tensor,)), dma((dp,)), dma((dp,)), dma((dp,)), dma((dp, tensor)),
+            pltpu.VMEM((dp, nblk * RANK, in_cols + out_cols), jnp.bfloat16),
+            dma((5,)), dma((tensor,)), dma((dp,)), dma((dp,)), dma((dp,)), dma((dp, tensor)),
             dma((dp - 1,)), dma((dp,)), dma((tensor - 1,)), dma((tensor,)),
-            dma((dp - 1,)), dma((dp,)), dma((dp - 1, chunks)), dma((dp + 1, chunks)),
+            dma((2, dp - 1)), dma((dp,)), dma((dp - 1, 2 * chunks)), dma((dp + 1, 2 * chunks)),
         ],
         compiler_params=pltpu.CompilerParams(
             collective_id=0, has_side_effects=True, vmem_limit_bytes=48 * 1024 * 1024

time: 146 us -> 136 us (0.932)
  the two profiles are of different devices: /device:TPU:17 before, /device:TPU:3 now
where the time goes in v2:
time: 136 us
  Pallas kernels  125 us (92%)
  local copies, waits for them, and re-layouts  10.1 us (7%)
    pallas_call x1, Pallas kernels, fused(): pl.pallas_call(functools.partial(fused_kernel, dp, tensor, chunks), out_s...  125 us
    unnamed x17, local copies, waits for them, and re-layouts  10.1 us

profile of v2, /device:TPU:3, one launch (start us, length us, event | category | flops | bytes accessed | tf_op | source)
XLA Modules:
  0.0 135.7 jit_solution(17474945208044651621)
XLA Ops:
  0.6 0.0 copy-start
  0.6 1.2 copy-done
  1.9 0.0 copy-start.1
  1.9 1.2 copy-done.1
  3.1 0.0 copy-start.2
  3.1 1.0 copy-done.2
  4.1 0.0 copy-start.3
  4.1 1.0 copy-done.3
  5.2 0.0 copy-start.4
  5.2 0.7 copy-done.4
  5.8 0.0 copy-start.5
  5.8 0.7 copy-done.5
  6.5 124.9 %shard_map.94 = (bf16[256,2048]{1,0:T(8,128)(2,1)S(1)}, f32[256,2048]{1,0:T(8,128)}, f32[256,1024]{1,0:T(8,128)S(1)}) custom-call(s32[8]{0:T(128)S(1)} %copy-done.4, s32[64]{0:T(128)S(1)} %copy-done.5, bf16[256,2048]{1,0:T(8,128)(2,1)S(1)} %copy-done, bf16[256,1024]{1,0:T(8,128)(2,1)S(1)} %copy-done.2, bf16[2048,1024]{1,0:T(8,128)(2,1)} %w_hbm.1, ...), custom_call_target="tpu_custom_call" | custom-call | flops 4294967296 | bytes 12582912 | tf_op jit(solution)/shard_map/pallas_call | solution.py:299
  131.4 0.0 copy-start.6
  131.4 1.0 copy.13
  132.4 1.0 copy-done.6
  133.4 1.3 copy.14
  134.7 1.0 copy.15
Async XLA Ops:
  0.6 1.2 copy-start
  1.9 1.2 copy-start.1
  3.1 1.0 copy-start.2
  4.1 1.0 copy-start.3
  5.2 0.7 copy-start.4
  5.8 0.7 copy-start.5
  131.4 2.0 %copy-start.6 = (f32[256,2048]{1,0:T(8,128)S(1)}, f32[256,2048]{1,0:T(8,128)}, u32[]{:S(2)}) copy-start(f32[256,2048]{1,0:T(8,128)} %get-tuple-element.7) | copy-start | bytes 6291460

commit v3 on v2

--- a/solution.py
+++ b/solution.py
@@ -326,7 +326,7 @@
             dma((2, dp - 1)), dma((dp,)), dma((dp - 1, 2 * chunks)), dma((dp + 1, 2 * chunks)),
         ],
         compiler_params=pltpu.CompilerParams(
-            collective_id=0, has_side_effects=True, vmem_limit_bytes=48 * 1024 * 1024
+            collective_id=0, has_side_effects=True, vmem_limit_bytes=58 * 1024 * 1024
         ),
         cost_estimate=pl.CostEstimate(
             flops=2 * dp * rows * in_cols * w.shape[1], bytes_accessed=12 * 1024 * 1024, transcendentals=0

time: 136 us -> 132 us (0.971)
  local copies, waits for them, and re-layouts: 10.1 us -> 5.38 us
    unnamed x17 -> x7, local copies, waits for them, and re-layouts: 10.1 us -> 5.38 us
where the time goes in v3:
time: 132 us
  Pallas kernels  126 us (95%)
  local copies, waits for them, and re-layouts  5.38 us (4%)
    pallas_call x1, Pallas kernels, fused(): pl.pallas_call(functools.partial(fused_kernel, dp, tensor, chunks), out_s...  126 us
    unnamed x7, local copies, waits for them, and re-layouts  5.38 us

profile of v3, /device:TPU:3, one launch (start us, length us, event | category | flops | bytes accessed | tf_op | source)
XLA Modules:
  0.0 131.7 jit_solution(1708556048392292305)
XLA Ops:
  0.6 125.7 %shard_map.94 = (bf16[256,2048]{1,0:T(8,128)(2,1)}, f32[256,2048]{1,0:T(8,128)}, f32[256,1024]{1,0:T(8,128)}) custom-call(s32[8]{0:T(128)} %block_ref.1, s32[64]{0:T(128)} %slot_ref.1, bf16[256,2048]{1,0:T(8,128)(2,1)} %acts_hbm.1, bf16[256,1024]{1,0:T(8,128)(2,1)} %og_hbm.1, bf16[2048,1024]{1,0:T(8,128)(2,1)} %w_hbm.1, bf16[16,16,2048]{2,1,0:T(8,128)(2,1)} %down_hbm.1, ...), custom_call_target="tpu_custom_call" | custom-call | flops 4294967296 | bytes 12582912 | tf_op jit(solution)/shard_map/pallas_call | solution.py:299
  126.3 0.0 copy-start
  126.3 2.5 %copy.13 = bf16[256,2048]{1,0:T(8,128)(2,1)} copy(bf16[256,2048]{1,0:T(8,128)(2,1)} %get-tuple-element.12) | data formatting | bytes 2097152
  128.8 0.0 copy-done
  128.8 0.0 copy-start.1
  128.8 1.3 %copy.14 = f32[16,16,2048]{2,1,0:T(8,128)} copy(f32[16,16,2048]{2,1,0:T(8,128)S(1)} %bitcast.2) | data formatting | bytes 4194304
  130.1 0.6 copy-done.1
  130.7 1.0 copy.15
Async XLA Ops:
  126.3 2.5 %copy-start = (f32[256,2048]{1,0:T(8,128)S(1)}, f32[256,2048]{1,0:T(8,128)}, u32[]{:S(2)}) copy-start(f32[256,2048]{1,0:T(8,128)} %get-tuple-element.7) | copy-start | bytes 6291460
  128.8 2.0 %copy-start.1 = (f32[256,1024]{1,0:T(8,128)S(1)}, f32[256,1024]{1,0:T(8,128)}, u32[]{:S(2)}) copy-start(f32[256,1024]{1,0:T(8,128)} %get-tuple-element.8) | copy-start | bytes 3145732

commit v4 on v3

--- a/solution.py
+++ b/solution.py
@@ -291,7 +291,7 @@
 def fused(dp, tensor, acts, og, w, down, up, blocks, slots):
     rows, in_cols = acts.shape
     out_cols = og.shape[1]
-    nslot, nblk, chunks = down.shape[0], rows // BLOCK_TOKENS, 4
+    nslot, nblk, chunks = down.shape[0], rows // BLOCK_TOKENS, 8
     width, half = in_cols // chunks, rows // 2
     vmem, smem = pl.BlockSpec(memory_space=pltpu.VMEM), pl.BlockSpec(memory_space=pltpu.SMEM)
     hbm = pl.BlockSpec(memory_space=pltpu.HBM)

time: 132 us -> 133 us (level)
  no operation moved by 1% of the time
where the time goes in v4:
time: 133 us; the launch traced here: 132 us
  Pallas kernels  126 us (95%)
  local copies, waits for them, and re-layouts  5.38 us (4%)
    pallas_call x1, Pallas kernels, fused(): pl.pallas_call(functools.partial(fused_kernel, dp, tensor, chunks), out_s...  126 us
    unnamed x7, local copies, waits for them, and re-layouts  5.38 us

profile of v4, /device:TPU:3, one launch (start us, length us, event | category | flops | bytes accessed | tf_op | source)
XLA Modules:
  0.0 132.4 jit_solution(157388191012877969)
XLA Ops:
  0.6 126.3 %shard_map.94 = (bf16[256,2048]{1,0:T(8,128)(2,1)}, f32[256,2048]{1,0:T(8,128)}, f32[256,1024]{1,0:T(8,128)}) custom-call(s32[8]{0:T(128)} %block_ref.1, s32[64]{0:T(128)} %slot_ref.1, bf16[256,2048]{1,0:T(8,128)(2,1)} %acts_hbm.1, bf16[256,1024]{1,0:T(8,128)(2,1)} %og_hbm.1, bf16[2048,1024]{1,0:T(8,128)(2,1)} %w_hbm.1, bf16[16,16,2048]{2,1,0:T(8,128)(2,1)} %down_hbm.1, ...), custom_call_target="tpu_custom_call" | custom-call | flops 4294967296 | bytes 12582912 | tf_op jit(solution)/shard_map/pallas_call | solution.py:299
  127.0 0.0 copy-start
  127.0 2.5 %copy.13 = bf16[256,2048]{1,0:T(8,128)(2,1)} copy(bf16[256,2048]{1,0:T(8,128)(2,1)} %get-tuple-element.12) | data formatting | bytes 2097152
  129.5 0.0 copy-done
  129.5 0.0 copy-start.1
  129.5 1.3 copy.14
  130.8 0.6 copy-done.1
  131.4 1.0 copy.15
Async XLA Ops:
  127.0 2.5 %copy-start = (f32[256,2048]{1,0:T(8,128)S(1)}, f32[256,2048]{1,0:T(8,128)}, u32[]{:S(2)}) copy-start(f32[256,2048]{1,0:T(8,128)} %get-tuple-element.7) | copy-start | bytes 6291460
  129.5 2.0 %copy-start.1 = (f32[256,1024]{1,0:T(8,128)S(1)}, f32[256,1024]{1,0:T(8,128)}, u32[]{:S(2)}) copy-start(f32[256,1024]{1,0:T(8,128)} %get-tuple-element.8) | copy-start | bytes 3145732
